TPU v7x, 32 devices: a whole 2x2x4 slice. The times are simulated.
32 devices in a mesh: groups: 2 (over y), gx: 4 (over x, core), gy: 4 (over z).
Axes of the slice: x: 2, y: 2, z: 4, core: 2. Of those that a mesh axis runs over, the one named last changes fastest.
Arguments:
- activations: bfloat16 [512, 8192], P('groups', ('gx', 'gy')), parts along dimension 0, may hold values from -6 to 6
- gate_up: bfloat16 [8192, 2, 26624], P('gx', None, 'gy'), may hold values from -0.0625 to 0.0625
Outputs:
- hidden: bfloat16 [512, 26624], P(('groups', 'gx'), 'gy'), parts along dimension 0
There are 2 independent parts, one for each index of `groups`. A program takes and returns all parts, laid end to end along the dimension named above; an argument that names none is the same for every part. Nothing has to cross between parts.
All inputs are finite; a program needn't handle non-finite values.
Results may differ from a plain program's by a relative error of at most 0.015.
Values may be sent and summed in bfloat16 or wider, within the bound.
A program may use at most 128 MiB of HBM per device.

v0:
```python
import jax
import jax.numpy as jnp
from jax import lax
from jax.sharding import PartitionSpec as P


def on_device(activations, gate_up):
    gathered = lax.all_gather(activations, "gy", axis=1, tiled=True)
    partial_value = jnp.einsum("rd,dkf->rkf", gathered, gate_up, preferred_element_type=jnp.float32)
    summed = lax.psum_scatter(
        partial_value.astype(jnp.bfloat16), "gx", scatter_dimension=0, tiled=True
    ).astype(jnp.float32)
    hidden = jax.nn.silu(summed[:, 0]) * summed[:, 1]
    return hidden.astype(jnp.bfloat16)


def solution(mesh):
    placed = (P("groups", ("gx", "gy")), P("gx", None, "gy"))
    return jax.shard_map(
        on_device, mesh=mesh, in_specs=placed, out_specs=P(("groups", "gx"), "gy"), check_vma=False
    )
```

profile of v0, /device:TPU:0, one launch (start us, length us, event | category | flops | bytes accessed | tf_op | source)
XLA Modules:
  0.0 145.6 jit_solution(9448690495994978441)
XLA Ops:
  6.5 0.0 all-gather.2.cloned.1.call-start
  6.5 0.7 all-gather.2.cloned.1.call-update
  7.3 0.0 reduce-scatter.2.cloned.1.call-start
  7.3 32.3 %all-gather.2.cloned.1.call-done = bf16[256,2048]{1,0:T(8,128)(2,1)} async-done(((bf16[256,512]{1,0:T(8,128)(2,1)}), bf16[256,2048]{1,0:T(8,128)(2,1)}) %all-gather.2.cloned.1.call-update) | async-done | bytes 1048592 | tf_op jit(solution)/shard_map/all_gather | solution.py:8
  39.6 34.4 %fusion.2 = bf16[256,2,6656]{2,0,1:T(8,128)(2,1)} fusion(bf16[2048,2,6656]{2,1,0:T(2,128)(2,1)} %param.3, bf16[256,2048]{1,0:T(8,128)(2,1)} %all-gather.2.cloned.1.call-done), kind=kOutput, calls=%fused_computation.2 | convolution fusion | flops 13962051584 | bytes 62390272 | tf_op jit(solution)/shard_map/rd,dkf->rkf/dot_general | solution.py:9
  74.0 0.0 reduce-scatter.2.cloned.1.call-update
  74.0 61.6 %reduce-scatter.2.cloned.1.call-done = bf16[64,2,6656]{2,0,1:T(8,128)(2,1)} async-done(((bf16[256,2,6656]{2,0,1:T(8,128)(2,1)}), bf16[64,2,6656]{2,0,1:T(8,128)(2,1)}) %reduce-scatter.2.cloned.1.call-update) | async-done | bytes 1703952 | tf_op jit(solution)/shard_map/reduce_scatter | solution.py:10
  135.6 1.8 %convert_element_type.10 = f32[64,2,6656]{2,0,1:T(8,128)S(1)} convert(bf16[64,2,6656]{2,0,1:T(8,128)(2,1)} %reduce-scatter.2.cloned.1.call-done) | non-fusion elementwise | flops 851968 | bytes 5111808 | tf_op jit(solution)/shard_map/convert_element_type | solution.py:12
  137.4 1.4 fusion.6
Async XLA Ops:
  6.5 33.1 %all-gather.2.cloned.1.call-start = ((), (), s32[]{:S(2)}) async-start(), calls=%async_computation.1 | async-start | bytes 1310720 | tf_op jit(solution)/shard_map/all_gather | solution.py:8
  7.3 128.4 %reduce-scatter.2.cloned.1.call-start = ((), (), s32[]{:S(2)}) async-start(), calls=%async_computation.2 | async-start | bytes 8519680 | tf_op jit(solution)/shard_map/reduce_scatter | solution.py:10
Sparse Core Ops, SparseCore 0:
  8.9 30.6 all-gather.1
  74.1 61.4 reduce-scatter.1
where the time goes:
time: 146 us
  waiting for transfers between devices  94.6 us (65%)
  matrix products  34.4 us (24%)
  between operations  13.4 us (9%)
  other arithmetic  3.13 us (2%)
    reduce_scatter x1, waiting for transfers between devices, on_device(): lax.psum_scatter(partial_value.astype(jnp.bfloat16), 'gx', scatter_dimens...  61.6 us
    dot_general x1, matrix products, on_device(): jnp.einsum('rd,dkf->rkf', gathered, gate_up, preferred_element_type=jnp.f...  34.4 us
    all_gather x1, waiting for transfers between devices, on_device(): gathered = lax.all_gather(activations, 'gy', axis=1, tiled=True)  32.3 us
  transfers between devices with their start and end apart: 2, of which 2 were waited for; matrix products, arithmetic and copies ran while one was open for 0% of the time, Pallas kernels for 0%

commit v1 on v0

v1 whole, which is shorter than its diff:
```python
import jax
import jax.numpy as jnp
from jax import lax
from jax.experimental import pallas as pl
from jax.experimental.pallas import tpu as pltpu
from jax.sharding import PartitionSpec as P

MESH = pl.DeviceIdType.MESH
TILE = 256
HALF = 128
RESIDENT = 14
STREAM = 4


def kernel(
    a, w, out, a_all, a2, wbuf, s1, r1, keep, s2, r2,
    wsem, ag_s, ag_r, s1_s, s1_r, s2_s, s2_r,
):
    nz = a_all.shape[0] + 1
    width = a.shape[1]
    block = a.shape[0] // 4
    depth = nz * width
    nt = s2.shape[0]
    resident, stream = min(RESIDENT, nt), STREAM
    cycle = nt - resident
    z, gx = lax.axis_index("gy"), lax.axis_index("gx")
    x, c = gx // 2, gx % 2
    core_peer = 2 * x + 1 - c
    chip_peer = 2 * (1 - x) + c

    def w_copies(tile, slot):
        return [
            pltpu.make_async_copy(w.at[:, 2 * tile + h], wbuf.at[slot, h], wsem.at[slot, h])
            for h in range(2)
        ]

    def load(tile, slot):
        for copy in w_copies(tile, slot):
            copy.start()

    def load_stream(m):
        load(resident + m % cycle, resident + m % stream)

    barrier = pltpu.get_barrier_semaphore()
    for i in range(1, nz):
        pl.semaphore_signal(barrier, inc=1, device_id={"gy": (z + i) % nz}, device_id_type=MESH)
    for peer in (core_peer, chip_peer):
        pl.semaphore_signal(barrier, inc=1, device_id={"gx": peer}, device_id_type=MESH)

    def load_first(t, carry):
        load(t, t)
        return carry

    lax.fori_loop(0, 2, load_first, 0)
    pl.semaphore_wait(barrier, nz + 1)

    def gather(i, phase):
        side = 1 - x if phase == 0 else x
        rows = pl.ds(pl.multiple_of(side * 2 * block, 2 * block), 2 * block)
        return pltpu.make_async_remote_copy(
            src_ref=a.at[rows],
            dst_ref=a_all.at[i - 1, rows],
            send_sem=ag_s.at[i - 1, phase],
            recv_sem=ag_r.at[i - 1, phase],
            device_id={"gy": (z + i) % nz},
            device_id_type=MESH,
        )

    for phase in range(2):
        for i in range(1, nz):
            gather(i, phase).start()
    lax.fori_loop(2, resident, load_first, 0)
    if cycle:
        for m in range(min(stream, 2 * cycle)):
            load_stream(m)

    feature = lax.broadcasted_iota(jnp.int32, (HALF, 4 * HALF), 0)
    place = lax.broadcasted_iota(jnp.int32, (HALF, 4 * HALF), 1)
    spread = (place == 2 * feature + jnp.where(place < 2 * HALF, 0, 2 * HALF + 1)).astype(jnp.bfloat16)

    def widen(phase):
        side = 1 - x if phase == 0 else x
        for i in range(nz):
            source = (z + nz - i) % nz
            if i:
                gather(i, phase).wait_recv()
            for q in range(2):
                core = c if q == 0 else 1 - c
                rows = pl.ds(pl.multiple_of((2 * side + core) * block, block), block)
                for j in range(width // HALF):
                    lanes = pl.ds(j * HALF, HALF)
                    piece = a[rows, lanes] if i == 0 else a_all[i - 1, rows, lanes]
                    both = jnp.dot(piece, spread, preferred_element_type=jnp.float32).astype(jnp.bfloat16)
                    to = pl.ds(pl.multiple_of(source * 2 * width + j * 2 * HALF, 2 * HALF), 2 * HALF)
                    a2[phase, pl.ds(q * 2 * block, block), to] = both[:, : 2 * HALF]
                    a2[phase, pl.ds(q * 2 * block + block, block), to] = both[:, 2 * HALF :]

    def to_core(i):
        return pltpu.make_async_remote_copy(
            src_ref=s1.at[i], dst_ref=r1.at[i], send_sem=s1_s.at[i], recv_sem=s1_r.at[i],
            device_id={"gx": core_peer}, device_id_type=MESH,
        )

    def to_chip(t):
        return pltpu.make_async_remote_copy(
            src_ref=s2.at[t], dst_ref=r2.at[t], send_sem=s2_s.at[t], recv_sem=s2_r.at[t],
            device_id={"gx": chip_peer}, device_id_type=MESH,
        )

    def chip_sum(i):
        to_core(i).wait_recv()
        return keep[i % 2] + r1[i].astype(jnp.float32)

    def pass_on(t):
        s2[t] = chip_sum(t).astype(jnp.bfloat16)
        to_chip(t).start()

    def finish(t):
        total = chip_sum(nt + t)
        to_chip(t).wait_recv()
        total = total + r2[t].astype(jnp.float32)
        gate, up = total[:block], total[block:]
        hidden = gate / (1.0 + jnp.exp(-gate)) * up
        out[:, pl.ds(pl.multiple_of(t * TILE, TILE), TILE)] = hidden.astype(jnp.bfloat16)

    def step(i, carry):
        phase = i // nt
        t = i % nt
        m = phase * cycle + t - resident
        held = t < resident
        slot = jnp.where(held, t, resident + (m + stream) % stream)

        @pl.when(jnp.logical_or(phase == 0, jnp.logical_not(held)))
        def arrive():
            for copy in w_copies(t, slot):
                copy.wait()

        weights = jnp.concatenate(
            [wbuf.at[slot, h].reshape(2 * depth, HALF)[...] for h in range(2)], axis=1
        )
        value = jnp.dot(a2[phase], weights, preferred_element_type=jnp.float32)
        s1[i] = value[2 * block :].astype(jnp.bfloat16)
        to_core(i).start()
        keep[i % 2] = value[: 2 * block]

        if cycle:
            @pl.when(jnp.logical_and(jnp.logical_not(held), m + stream < 2 * cycle))
            def refill():
                load_stream(m + stream)

        @pl.when(jnp.logical_and(i >= 1, i <= nt))
        def send():
            pass_on(i - 1)

        @pl.when(i > nt)
        def done():
            finish(i - 1 - nt)

        return carry

    widen(0)
    lax.fori_loop(0, nt, step, 0)
    widen(1)
    lax.fori_loop(nt, 2 * nt, step, 0)
    finish(nt - 1)

    def drain(t, carry):
        to_core(t).wait_send()
        to_core(nt + t).wait_send()
        to_chip(t).wait_send()
        return carry

    lax.fori_loop(0, nt, drain, 0)
    for phase in range(2):
        for i in range(1, nz):
            gather(i, phase).wait_send()


def fused(nz, activations, gate_up):
    rows, width = activations.shape
    depth, pair, columns = gate_up.shape
    nt = columns // TILE
    weights = gate_up.reshape(depth, pair, columns // HALF, HALF).transpose(0, 2, 1, 3)
    slots = min(RESIDENT, nt) + STREAM
    half = rows // 2
    dma = pltpu.SemaphoreType.DMA
    return pl.pallas_call(
        kernel,
        out_shape=jax.ShapeDtypeStruct((rows // 4, columns), jnp.bfloat16),
        in_specs=[
            pl.BlockSpec(memory_space=pltpu.VMEM),
            pl.BlockSpec(memory_space=pl.ANY),
        ],
        out_specs=pl.BlockSpec(memory_space=pltpu.VMEM),
        scratch_shapes=[
            pltpu.VMEM((nz - 1, rows, width), jnp.bfloat16),
            pltpu.VMEM((2, rows, 2 * depth), jnp.bfloat16),
            pltpu.VMEM((slots, 2, depth, pair, HALF), jnp.bfloat16),
            pltpu.VMEM((2 * nt, half, TILE), jnp.bfloat16),
            pltpu.VMEM((2 * nt, half, TILE), jnp.bfloat16),
            pltpu.VMEM((2, half, TILE), jnp.float32),
            pltpu.VMEM((nt, half, TILE), jnp.bfloat16),
            pltpu.VMEM((nt, half, TILE), jnp.bfloat16),
            dma((slots, 2)),
            dma((nz - 1, 2)),
            dma((nz - 1, 2)),
            dma((2 * nt,)),
            dma((2 * nt,)),
            dma((nt,)),
            dma((nt,)),
        ],
        compiler_params=pltpu.CompilerParams(
            collective_id=0, has_side_effects=True, vmem_limit_bytes=60 * 2**20
        ),
    )(activations, weights)


def plain(activations, gate_up):
    gathered = lax.all_gather(activations, "gy", axis=1, tiled=True)
    partial_value = jnp.einsum("rd,dkf->rkf", gathered, gate_up, preferred_element_type=jnp.float32)
    summed = lax.psum_scatter(
        partial_value.astype(jnp.bfloat16), "gx", scatter_dimension=0, tiled=True
    ).astype(jnp.float32)
    hidden = jax.nn.silu(summed[:, 0]) * summed[:, 1]
    return hidden.astype(jnp.bfloat16)


def solution(mesh):
    nx, nz = mesh.shape["gx"], mesh.shape["gy"]

    def on_device(activations, gate_up):
        width, columns = activations.shape[1], gate_up.shape[2]
        if nx == 4 and nz > 1 and width % HALF == 0 and columns % TILE == 0:
            return fused(nz, activations, gate_up)
        return plain(activations, gate_up)

    placed = (P("groups", ("gx", "gy")), P("gx", None, "gy"))
    return jax.shard_map(
        on_device, mesh=mesh, in_specs=placed, out_specs=P(("groups", "gx"), "gy"), check_vma=False
    )
```

time: 146 us -> 94.4 us (0.65)
  the two profiles are of different devices: /device:TPU:0 before, /device:TPU:27 now
where the time goes in v1:
time: 94.4 us; the launch traced here: 94.2 us
  Pallas kernels  92.1 us (98%)
  local copies, waits for them, and re-layouts  2.11 us (2%)
    pallas_call x1, Pallas kernels, fused(): pl.pallas_call(kernel, out_shape=jax.ShapeDtypeStruct((rows // 4, columns...  92.1 us
    unnamed x1, local copies, waits for them, and re-layouts  2.11 us

profile of v1, /device:TPU:27, one launch (start us, length us, event | category | flops | bytes accessed | tf_op | source)
XLA Modules:
  0.0 94.2 jit_solution(7532718272135098128)
XLA Ops:
  0.0 92.1 %shard_map.28 = bf16[64,6656]{1,0:T(8,128)(2,1)} custom-call(bf16[256,512]{1,0:T(8,128)(2,1)} %a.1, bf16[2048,52,2,128]{3,2,1,0:T(2,128)(2,1)} %bitcast.3), custom_call_target="tpu_custom_call" | custom-call | tf_op jit(solution)/shard_map/pallas_call | solution.py:187
  92.1 2.1 %copy.4 = bf16[64,6656]{1,0:T(8,128)(2,1)} copy(bf16[64,6656]{1,0:T(8,128)(2,1)} %shard_map.28) | data formatting | bytes 1703936

commit v2 on v1

v2 whole, which is shorter than its diff:
```python
import jax
import jax.numpy as jnp
from jax import lax
from jax.experimental import pallas as pl
from jax.experimental.pallas import tpu as pltpu
from jax.sharding import PartitionSpec as P

MESH = pl.DeviceIdType.MESH
TILE = 512
HALF = 128
PARTS = TILE // HALF
SLOTS = 9
LAG = 4


def kernel(
    a, w, out, a_all, a2, wbuf, s1, r1, keep, near, s2, r2,
    wsem, ag_s, ag_r, s1_s, s1_r, s2_s, s2_r,
):
    nz = a_all.shape[0] + 1
    width = a.shape[1]
    block = a.shape[0] // 4
    depth = nz * width
    nt = s2.shape[0]
    slots = wbuf.shape[0]
    z, gx = lax.axis_index("gy"), lax.axis_index("gx")
    x, c = gx // 2, gx % 2
    core_peer = 2 * x + 1 - c
    chip_peer = 2 * (1 - x) + c

    def w_copies(tile):
        slot = tile % slots
        return [
            pltpu.make_async_copy(w.at[:, PARTS * tile + h], wbuf.at[slot, h], wsem.at[slot, h])
            for h in range(PARTS)
        ]

    def load(tile):
        for copy in w_copies(tile):
            copy.start()

    barrier = pltpu.get_barrier_semaphore()
    for i in range(1, nz):
        pl.semaphore_signal(barrier, inc=1, device_id={"gy": (z + i) % nz}, device_id_type=MESH)
    for peer in (core_peer, chip_peer):
        pl.semaphore_signal(barrier, inc=1, device_id={"gx": peer}, device_id_type=MESH)

    def load_first(t, carry):
        load(t)
        return carry

    lax.fori_loop(0, 1, load_first, 0)
    pl.semaphore_wait(barrier, nz + 1)

    def gather(i, phase):
        side = 1 - x if phase == 0 else x
        rows = pl.ds(pl.multiple_of(side * 2 * block, 2 * block), 2 * block)
        return pltpu.make_async_remote_copy(
            src_ref=a.at[rows],
            dst_ref=a_all.at[i - 1, rows],
            send_sem=ag_s.at[i - 1, phase],
            recv_sem=ag_r.at[i - 1, phase],
            device_id={"gy": (z + i) % nz},
            device_id_type=MESH,
        )

    for phase in range(2):
        for i in range(1, nz):
            gather(i, phase).start()
    lax.fori_loop(1, slots, load_first, 0)

    feature = lax.broadcasted_iota(jnp.int32, (HALF, 4 * HALF), 0)
    place = lax.broadcasted_iota(jnp.int32, (HALF, 4 * HALF), 1)
    spread = (place == 2 * feature + jnp.where(place < 2 * HALF, 0, 2 * HALF + 1)).astype(jnp.bfloat16)

    def widen(phase):
        side = 1 - x if phase == 0 else x
        for i in range(nz):
            source = (z + nz - i) % nz
            if i:
                gather(i, phase).wait_recv()
            for q in range(2):
                core = c if q == 0 else 1 - c
                rows = pl.ds(pl.multiple_of((2 * side + core) * block, block), block)
                for j in range(width // HALF):
                    lanes = pl.ds(j * HALF, HALF)
                    piece = a[rows, lanes] if i == 0 else a_all[i - 1, rows, lanes]
                    both = jnp.dot(piece, spread, preferred_element_type=jnp.float32).astype(jnp.bfloat16)
                    to = pl.ds(pl.multiple_of(source * 2 * width + j * 2 * HALF, 2 * HALF), 2 * HALF)
                    a2[pl.ds((2 * phase + q) * 2 * block, block), to] = both[:, : 2 * HALF]
                    a2[pl.ds((2 * phase + q) * 2 * block + block, block), to] = both[:, 2 * HALF :]

    def to_core(i):
        return pltpu.make_async_remote_copy(
            src_ref=s1.at[i], dst_ref=r1.at[i], send_sem=s1_s.at[i], recv_sem=s1_r.at[i],
            device_id={"gx": core_peer}, device_id_type=MESH,
        )

    def to_chip(t):
        return pltpu.make_async_remote_copy(
            src_ref=s2.at[t], dst_ref=r2.at[t], send_sem=s2_s.at[t], recv_sem=s2_r.at[t],
            device_id={"gx": chip_peer}, device_id_type=MESH,
        )

    def pass_on(t):
        to_core(t).wait_recv()
        total = keep[t % 2] + r1[t].astype(jnp.float32)
        s2[t] = total[: 2 * block].astype(jnp.bfloat16)
        to_chip(t).start()
        near[t] = total[2 * block :]

    def finish(t):
        to_chip(t).wait_recv()
        total = near[t] + r2[t].astype(jnp.float32)
        gate, up = total[:block], total[block:]
        hidden = gate / (1.0 + jnp.exp(-gate)) * up
        out[:, pl.ds(pl.multiple_of(t * TILE, TILE), TILE)] = hidden.astype(jnp.bfloat16)

    def step(t, carry):
        for copy in w_copies(t):
            copy.wait()
        slot = t % slots
        weights = jnp.concatenate(
            [wbuf.at[slot, h].reshape(2 * depth, HALF)[...] for h in range(PARTS)], axis=1
        )
        value = jnp.dot(a2[...], weights, preferred_element_type=jnp.float32)
        for side in range(2):
            own = pl.ds(side * 2 * block, 2 * block)
            at = side * 4 * block
            keep[t % 2, own] = value[at : at + 2 * block]
            s1[t, own] = value[at + 2 * block : at + 4 * block].astype(jnp.bfloat16)
        to_core(t).start()

        @pl.when(t + slots < nt)
        def refill():
            load(t + slots)

        @pl.when(t >= 1)
        def send():
            pass_on(t - 1)

        @pl.when(t >= LAG)
        def done():
            finish(t - LAG)

        return carry

    widen(0)
    widen(1)
    lax.fori_loop(0, nt, step, 0)
    pass_on(nt - 1)

    def rest(t, carry):
        finish(t)
        return carry

    lax.fori_loop(max(nt - LAG, 0), nt, rest, 0)

    def drain(t, carry):
        to_core(t).wait_send()
        to_chip(t).wait_send()
        return carry

    lax.fori_loop(0, nt, drain, 0)
    for phase in range(2):
        for i in range(1, nz):
            gather(i, phase).wait_send()


def fused(nz, activations, gate_up):
    rows, width = activations.shape
    depth, pair, columns = gate_up.shape
    nt = columns // TILE
    weights = gate_up.reshape(depth, pair, columns // HALF, HALF).transpose(0, 2, 1, 3)
    slots = min(SLOTS, nt)
    dma = pltpu.SemaphoreType.DMA
    return pl.pallas_call(
        kernel,
        out_shape=jax.ShapeDtypeStruct((rows // 4, columns), jnp.bfloat16),
        in_specs=[
            pl.BlockSpec(memory_space=pltpu.VMEM),
            pl.BlockSpec(memory_space=pl.ANY),
        ],
        out_specs=pl.BlockSpec(memory_space=pltpu.VMEM),
        scratch_shapes=[
            pltpu.VMEM((nz - 1, rows, width), jnp.bfloat16),
            pltpu.VMEM((2 * rows, 2 * depth), jnp.bfloat16),
            pltpu.VMEM((slots, PARTS, depth, pair, HALF), jnp.bfloat16),
            pltpu.VMEM((nt, rows, TILE), jnp.bfloat16),
            pltpu.VMEM((nt, rows, TILE), jnp.bfloat16),
            pltpu.VMEM((2, rows, TILE), jnp.float32),
            pltpu.VMEM((nt, rows // 2, TILE), jnp.float32),
            pltpu.VMEM((nt, rows // 2, TILE), jnp.bfloat16),
            pltpu.VMEM((nt, rows // 2, TILE), jnp.bfloat16),
            dma((slots, PARTS)),
            dma((nz - 1, 2)),
            dma((nz - 1, 2)),
            dma((nt,)),
            dma((nt,)),
            dma((nt,)),
            dma((nt,)),
        ],
        compiler_params=pltpu.CompilerParams(
            collective_id=0, has_side_effects=True, vmem_limit_bytes=60 * 2**20
        ),
    )(activations, weights)


def plain(activations, gate_up):
    gathered = lax.all_gather(activations, "gy", axis=1, tiled=True)
    partial_value = jnp.einsum("rd,dkf->rkf", gathered, gate_up, preferred_element_type=jnp.float32)
    summed = lax.psum_scatter(
        partial_value.astype(jnp.bfloat16), "gx", scatter_dimension=0, tiled=True
    ).astype(jnp.float32)
    hidden = jax.nn.silu(summed[:, 0]) * summed[:, 1]
    return hidden.astype(jnp.bfloat16)


def solution(mesh):
    nx, nz = mesh.shape["gx"], mesh.shape["gy"]

    def on_device(activations, gate_up):
        width, columns = activations.shape[1], gate_up.shape[2]
        if nx == 4 and nz > 1 and width % HALF == 0 and columns % TILE == 0:
            return fused(nz, activations, gate_up)
        return plain(activations, gate_up)

    placed = (P("groups", ("gx", "gy")), P("gx", None, "gy"))
    return jax.shard_map(
        on_device, mesh=mesh, in_specs=placed, out_specs=P(("groups", "gx"), "gy"), check_vma=False
    )
```

time: 94.4 us -> 75.1 us (0.80)
  the two profiles are of different devices: /device:TPU:27 before, /device:TPU:0 now
where the time goes in v2:
time: 75.1 us; the launch traced here: 74.9 us
  Pallas kernels  72.8 us (97%)
  local copies, waits for them, and re-layouts  2.11 us (3%)
    pallas_call x1, Pallas kernels, fused(): pl.pallas_call(kernel, out_shape=jax.ShapeDtypeStruct((rows // 4, columns...  72.8 us
    unnamed x1, local copies, waits for them, and re-layouts  2.11 us

profile of v2, /device:TPU:0, one launch (start us, length us, event | category | flops | bytes accessed | tf_op | source)
XLA Modules:
  0.0 74.9 jit_solution(12762989414964059377)
XLA Ops:
  0.0 72.8 %shard_map.28 = bf16[64,6656]{1,0:T(8,128)(2,1)} custom-call(bf16[256,512]{1,0:T(8,128)(2,1)} %a.1, bf16[2048,52,2,128]{3,2,1,0:T(2,128)(2,1)} %bitcast.3), custom_call_target="tpu_custom_call" | custom-call | tf_op jit(solution)/shard_map/pallas_call | solution.py:177
  72.8 2.1 %copy.4 = bf16[64,6656]{1,0:T(8,128)(2,1)} copy(bf16[64,6656]{1,0:T(8,128)(2,1)} %shard_map.28) | data formatting | bytes 1703936
